TPU v7x, 256 devices: a whole 4x4x8 slice. The times are simulated.
256 devices in a mesh: row: 16 (over x, z_hi, core), col: 16 (over y, z_lo).
Axes of the slice: x: 4, y: 4, z: 8 (z_hi: 2, z_lo: 4; z = z_hi * 4 + z_lo), core: 2. Of those that a mesh axis runs over, the one named last changes fastest.
Arguments:
- surface: bfloat16 [2048, 118784], P(None, ('row', 'col')), may hold values from -24 to 24
- eigvec: bfloat16 [118784, 2048], P('row', 'col'), may hold values from -0.015625 to 0.015625
- eig_energy: float32 [2048], replicated, may hold values from 1 to 10
- energies: float32 [8], replicated, may hold values from -1 to 0.5
Outputs:
- amplitudes: float32 [2048, 2048], P('row', 'col')
- rmatrix: float32 [8, 2048, 2048], P(None, 'row', 'col')
All inputs are finite; a program needn't handle non-finite values.
Results may differ from a plain program's by a relative error of at most 0.0003.
Values may be sent and summed in bfloat16 or wider, within the bound.
A program may use at most 64 MiB of HBM per device.

v0:
```python
import math

import jax
import jax.numpy as jnp
from jax import lax
from jax.sharding import PartitionSpec as P


def spread(block, axis, source):
    block = jnp.where(lax.axis_index(axis) == source, block, jnp.zeros_like(block))
    return lax.psum(block, axis)


def local(surface, eigvec, eig_energy, energies):
    channels = surface.shape[0]
    width = eig_energy.shape[0]
    rows_all = lax.all_to_all(eigvec, "col", split_axis=0, concat_axis=1, tiled=True)
    sliver = lax.psum_scatter(
        jnp.dot(surface, rows_all, preferred_element_type=jnp.float32),
        ("row", "col"),
        scatter_dimension=0,
        tiled=True,
    )
    panel_own = lax.all_gather(sliver, "col", axis=0, tiled=True)
    col_index = lax.axis_index("col")
    col_width = width // lax.axis_size("col")
    amplitudes = lax.dynamic_slice_in_dim(panel_own, col_index * col_width, col_width, 1)
    own_rows = panel_own.shape[0]
    other_rows = channels // lax.axis_size("col")
    first = col_index * other_rows
    received = spread(panel_own, "row", first // own_rows)
    poles = 1.0 / (eig_energy[None, :] - energies[:, None])
    factor = 1.0 / math.sqrt(width)

    def one_energy(weights):
        scaled = panel_own * weights[None, :]
        product = lax.dot_general(
            scaled,
            received,
            (((1,), (1,)), ((), ())),
            precision=lax.Precision.HIGHEST,
            preferred_element_type=jnp.float32,
        )
        return product * factor

    rmatrix = lax.map(one_energy, poles)
    return (amplitudes, rmatrix)


def solution(mesh):
    in_specs = (P(None, ("row", "col")), P("row", "col"), P(), P())
    out_specs = (P("row", "col"), P(None, "row", "col"))
    return jax.shard_map(local, mesh=mesh, in_specs=in_specs, out_specs=out_specs, check_vma=False)
```

profile of v0, /device:TPU:7, one launch (start us, length us, event | category | flops | bytes accessed | tf_op | source)
XLA Modules:
  0.0 1654.6 jit_solution(17368588393061046118)
XLA Ops:
  7.2 0.0 copy-start
  7.2 0.0 reduce-scatter.2.cloned.1.call-start
  7.2 53.7 %all_to_all.19 = bf16[16,464,128]{2,1,0:T(8,128)(2,1)S(1)} all-to-all(bf16[16,464,128]{2,1,0:T(8,128)(2,1)} %bitcast.22), channel_id=1, replica_groups=mesh['row'=16,'col'=16] {'col'}, dimensions={0} | all-to-all | bytes 3801088 | tf_op jit(solution)/shard_map/all_to_all | solution.py:17
  60.9 0.0 copy-done
  60.9 8.2 fusion.4
  69.1 0.0 reduce-scatter.2.cloned.1.call-update
  69.2 0.0 copy-start.2
  69.2 0.0 copy-start.3
  69.2 0.0 all-gather.2.cloned.1.call-start
  69.2 1186.7 %reduce-scatter.2.cloned.1.call-done = f32[8,2048]{1,0:T(8,128)} async-done(((f32[2048,2048]{1,0:T(8,128)}), f32[8,2048]{1,0:T(8,128)}) %reduce-scatter.2.cloned.1.call-update) | async-done | bytes 65552 | tf_op jit(solution)/shard_map/reduce_scatter | solution.py:18
  1255.9 0.0 all-gather.2.cloned.1.call-update
  1255.9 0.0 all-reduce.2.cloned.1.call-start
  1256.0 178.6 %all-gather.2.cloned.1.call-done = f32[128,2048]{1,0:T(8,128)} async-done(((f32[8,2048]{1,0:T(8,128)}), f32[128,2048]{1,0:T(8,128)}) %all-gather.2.cloned.1.call-update) | async-done | bytes 1048592 | tf_op jit(solution)/shard_map/all_gather | solution.py:24
  1434.6 0.0 copy-start.1
  1434.6 1.1 broadcast_select_fusion
  1435.7 0.0 all-reduce.2.cloned.1.call-update
  1435.7 0.0 copy-done.2
  1435.7 0.0 copy-done.3
  1435.7 0.1 subtract_divide_fusion
  1435.8 0.4 copy-done.1
  1436.2 0.6 constant_dynamic-slice_fusion.1
  1436.8 188.0 %all-reduce.2.cloned.1.call-done = f32[128,2048]{1,0:T(8,128)} async-done(((f32[128,2048]{1,0:T(8,128)}), f32[128,2048]{1,0:T(8,128)}) %all-reduce.2.cloned.1.call-update) | async-done | bytes 1048592 | tf_op jit(solution)/shard_map/psum | solution.py:11
  1624.8 23.2 %while.10 = (s32[]{:T(128)}, f32[8,128,128]{2,1,0:T(8,128)}, f32[8,2048]{1,0:T(8,128)S(1)}, f32[128,2048]{1,0:T(8,128)S(1)}, f32[128,2048]{1,0:T(8,128)}, /*index=5*/s32[]{:T(128)}) while((s32[]{:T(128)}, f32[8,128,128]{2,1,0:T(8,128)}, f32[8,2048]{1,0:T(8,128)S(1)}, f32[128,2048]{1,0:T(8,128)S(1)}, f32[128,2048]{1,0:T(8,128)}, ...), condition=%wide.region_3.4_spmd, body=%wide.region_2.3_spmd.sunk | while | flops 402931712 | bytes 2187349 | solution.py:46
  1624.9 2.9 fusion.15
  1627.8 2.9 fusion.15
  1630.7 2.9 fusion.15
  1633.6 2.9 fusion.15
  1636.5 2.9 fusion.15
  1639.4 2.9 fusion.15
  1642.3 2.9 fusion.15
  1645.2 2.9 fusion.15
  (9 shorter events, 0.1 us)
Async XLA Ops:
  7.2 53.8 %copy-start = (bf16[2048,464]{0,1:T(8,128)(2,1)S(1)}, bf16[2048,464]{0,1:T(8,128)(2,1)}, u32[]{:S(2)}) copy-start(bf16[2048,464]{0,1:T(8,128)(2,1)} %param.6) | copy-start | bytes 5701636
  7.2 1248.7 %reduce-scatter.2.cloned.1.call-start = ((), (), s32[]{:S(2)}) async-start(), calls=%async_computation.2 | async-start | bytes 16842752 | tf_op jit(solution)/shard_map/reduce_scatter | solution.py:18
  69.2 1366.6 %copy-start.2 = (f32[2048]{0:T(1024)S(1)}, f32[2048]{0:T(1024)}, u32[]{:S(2)}) copy-start(f32[2048]{0:T(1024)} %param.8) | copy-start | bytes 24580
  69.2 1366.6 %copy-start.3 = (f32[8]{0:T(128)S(1)}, f32[8]{0:T(128)}, u32[]{:S(2)}) copy-start(f32[8]{0:T(128)} %param.9) | copy-start | bytes 100
  69.2 1365.4 %all-gather.2.cloned.1.call-start = ((), (), s32[]{:S(2)}) async-start(), calls=%async_computation.3 | async-start | bytes 1114112 | tf_op jit(solution)/shard_map/all_gather | solution.py:24
  1255.9 368.9 %all-reduce.2.cloned.1.call-start = ((), (), s32[]{:S(2)}) async-start(), calls=%async_computation.4 | async-start | bytes 2097152 | tf_op jit(solution)/shard_map/psum | solution.py:11
  1434.6 1.6 copy-start.1
Sparse Core Ops, SparseCore 0:
  69.3 1186.5 reduce-scatter.1
  1257.8 176.7 all-gather.1
  1437.4 187.3 all-reduce.1
where the time goes:
time: 1660 us; the launch traced here: 1650 us
  waiting for transfers between devices  1550 us (93%)
  blocking collectives  53.7 us (3%)
  matrix products  31.3 us (2%)
    reduce_scatter x1, waiting for transfers between devices, local(): lax.psum_scatter(jnp.dot(surface, rows_all, preferred_element_type=jnp.fl...  1190 us
    psum x1, waiting for transfers between devices, spread(): return lax.psum(block, axis)  188 us
    all_gather x1, waiting for transfers between devices, local(): panel_own = lax.all_gather(sliver, 'col', axis=0, tiled=True)  179 us
    all_to_all x1, blocking collectives, local(): lax.all_to_all(eigvec, 'col', split_axis=0, concat_axis=1, tiled=True)  53.7 us
  transfers between devices with their start and end apart: 3, of which 3 were waited for; matrix products, arithmetic and copies ran while one was open for 0% of the time, Pallas kernels for 0%

commit v1 on v0

v1 whole, which is shorter than its diff:
```python
import functools
import math

import jax
import jax.numpy as jnp
from jax import lax
from jax.experimental import pallas as pl
from jax.experimental.pallas import tpu as pltpu
from jax.sharding import PartitionSpec as P

MESH = pl.DeviceIdType.MESH
XR = (0, 40)
YR = (40, 48)
ZR = (88, 40)
XY = XR[1] + YR[1]


def rows(part):
    return pl.ds(part[0], part[1])


def copy_to(device, src, dst, send, recv):
    return pltpu.make_async_remote_copy(
        src_ref=src, dst_ref=dst, send_sem=send, recv_sem=recv, device_id=device, device_id_type=MESH
    )


def add_into(dst, *srcs):
    shape = dst.shape
    if len(shape) == 2:
        total = dst[...]
        for s in srcs:
            total = total + s[...]
        dst[...] = total
        return
    lead = shape[:-2]
    count = math.prod(lead)

    def body(i, carry):
        at = (i,) if len(lead) == 1 else (i // lead[1], i % lead[1])
        total = dst[at]
        for s in srcs:
            total = total + s[at]
        dst[at] = total
        return carry

    lax.fori_loop(0, count, body, 0)


class Ring4:
    def __init__(self, at, plus, minus, chunk, far, near, send, recv):
        self.at, self.chunk, self.near = at, chunk, near
        up, down, across = (at + 1) % 4, (at + 3) % 4, (at + 2) % 4
        self.up, self.down, self.far = up, down, far
        c = functools.partial
        self.p1 = copy_to(plus, chunk(across, 0), far.at[0], send.at[0], recv.at[0])
        self.m1 = copy_to(minus, chunk(across, 1), far.at[1], send.at[1], recv.at[1])
        self.p2 = copy_to(plus, chunk(up, 1), near.at[0, 1], send.at[2], recv.at[2])
        self.m2 = copy_to(minus, chunk(down, 0), near.at[1, 0], send.at[3], recv.at[3])
        self.p3 = copy_to(plus, chunk(up, 0), near.at[0, 0], send.at[4], recv.at[4])
        self.m3 = copy_to(minus, chunk(down, 1), near.at[1, 1], send.at[5], recv.at[5])

    def start(self):
        for c in (self.p1, self.m1, self.p2, self.m2):
            c.start()

    def middle(self):
        self.p1.wait_recv()
        add_into(self.chunk(self.up, 0), self.far.at[0])
        self.p3.start()
        self.m1.wait_recv()
        add_into(self.chunk(self.down, 1), self.far.at[1])
        self.m3.start()

    def finish(self):
        for c in (self.p2, self.m2, self.p3, self.m3):
            c.wait_recv()
        for h in range(2):
            add_into(self.chunk(self.at, h), self.near.at[0, h], self.near.at[1, h])

    def close(self):
        for c in (self.p1, self.m1, self.p2, self.m2, self.p3, self.m3):
            c.wait_send()


class Ring8:
    def __init__(self, at, plus, minus, chunk, slots, send, recv):
        self.at, self.chunk, self.slots = at, chunk, slots
        self.copies, self.held = [], []
        for s in range(7):
            k = 4 - (s + 1) // 2
            h = 0 if s % 2 == 0 else 1
            pair, held = [], []
            for way, device in ((0, plus), (1, minus)):
                i = (at + k) % 8 if way == 0 else (at + 8 - k) % 8
                half = h if way == 0 else 1 - h
                view = chunk(i, half)
                held.append(view)
                pair.append(copy_to(device, view, slots.at[way, s], send.at[way, s], recv.at[way, s]))
            self.copies.append(pair)
            self.held.append(held)

    def start(self):
        for s in range(2):
            for c in self.copies[s]:
                c.start()

    def step(self, s):
        for way in range(2):
            self.copies[s - 2][way].wait_recv()
            add_into(self.held[s][way], self.slots.at[way, s - 2])
            self.copies[s][way].start()

    def finish(self):
        for s in (5, 6):
            for way in range(2):
                self.copies[s][way].wait_recv()
        add_into(self.chunk(self.at, 0), self.slots.at[0, 6], self.slots.at[1, 5])
        add_into(self.chunk(self.at, 1), self.slots.at[0, 5], self.slots.at[1, 6])

    def close(self):
        for pair in self.copies:
            for c in pair:
                c.wait_send()


def kernel(
    surf, eig, levels, energies, amp_out, r_out,
    s_buf, v_buf, part, xfar, xnear, yfar, ynear, zslot, x2far, x2near, y2far, y2near, w2far, w2near,
    z3, y3, ar, ac, pole,
    loc_sem, s_sem, a_send, a_recv, f_send, f_recv,
    x_sem, y_sem, z_sem, x2_sem, y2_sem, w2_sem, z3_sem, y3_sem, t1_sem, t1y_sem, t2_send, t2_recv, t3_sem,
):
    row, col = lax.axis_index("row"), lax.axis_index("col")
    x, zhi, core = row // 4, (row // 2) % 2, row % 2
    y, zlo = col // 4, col % 4
    z = zhi * 4 + zlo
    other = (row + 1 - 2 * core, col)

    def at_x(i):
        return ((i % 4) * 4 + zhi * 2 + core, col)

    def at_y(i):
        return (row, (i % 4) * 4 + zlo)

    def at_z(i):
        i = i % 8
        return (x * 4 + (i // 4) * 2 + core, y * 4 + i % 4)

    load_s = pltpu.make_async_copy(surf.at[:, core], s_buf.at[0], loc_sem.at[0])
    load_s.start()
    load_v = pltpu.make_async_copy(eig.at[col], v_buf.at[0, 0], loc_sem.at[1])
    load_v.start()

    barrier = pltpu.get_barrier_semaphore()

    def greet(device):
        pl.semaphore_signal(barrier, inc=1, device_id=device, device_id_type=MESH)

    def greet_col(j, carry):
        greet((row, ((y + j // 4) % 4) * 4 + (zlo + j % 4) % 4))
        return carry

    lax.fori_loop(1, 16, greet_col, 0)
    greet(other)
    greet(at_x(x + 1))
    greet(at_x(x + 3))

    def greet_z(j, carry):
        greet((x * 4 + (1 - zhi) * 2 + core, y * 4 + j))
        return carry

    lax.fori_loop(0, 4, greet_z, 0)

    def greet_t2(j, carry):
        source = 2 * j + core

        @pl.when(jnp.logical_or(row != col, source != col))
        def _():
            greet((col, source))

        return carry

    lax.fori_loop(0, 8, greet_t2, 0)
    diagonal = row == col
    pl.semaphore_wait(barrier, jnp.where(diagonal, 29, 30))

    def a2a(j):
        dest = ((y + j % 4) % 4) * 4 + (zlo + j // 4) % 4
        return copy_to((row, dest), eig.at[dest], v_buf.at[0, j], a_send.at[j], a_recv.at[j])

    def order(i):
        return jnp.where(i == 0, 0, (i + 2) % 15 + 1)

    def send_a2a(i, carry):
        a2a(order(i)).start()
        return carry

    lax.fori_loop(1, 16, send_a2a, 0)
    give_s = copy_to(other, surf.at[:, 1 - core], s_buf.at[1], s_sem.at[0], s_sem.at[1])
    give_s.start()

    pole[...] = (1.0 / math.sqrt(2048.0)) / (levels[...] - energies[...])

    def forward(j):
        return copy_to(other, v_buf.at[0, j], v_buf.at[1, j], f_send.at[j], f_recv.at[j])

    load_v.wait()
    forward(0).start()
    load_s.wait()
    give_s.wait_recv()

    def multiply(j):
        forward(j).wait_recv()
        ys, zs = (y + 4 - j % 4) % 4, (zlo + 4 - j // 4) % 4
        width = s_buf.shape[-1]
        got = jnp.dot(s_buf[0].reshape(1024, width), v_buf[0, j], preferred_element_type=jnp.float32)
        got += jnp.dot(s_buf[1].reshape(1024, width), v_buf[1, j], preferred_element_type=jnp.float32)
        got = got.reshape(4, 2, 128, 128)
        for xi in range(4):
            for zh in range(2):
                part[xi, ys, zh * 4 + zs] = got[xi, zh]

    def take(i, carry):
        j = order(i)

        @pl.when(i < 16)
        def _():
            a2a(j).wait_recv()
            forward(j).start()

        multiply(order(i - 1))
        return carry

    lax.fori_loop(1, 17, take, 0)

    ring_x = Ring4(x, at_x(x + 1), at_x(x + 3), lambda i, h: part.at[i, :, pl.ds(4 * h, 4), rows(XR)],
                   xfar, xnear, x_sem.at[0], x_sem.at[1])
    ring_y = Ring4(y, at_y(y + 1), at_y(y + 3), lambda i, h: part.at[:, i, pl.ds(4 * h, 4), rows(YR)],
                   yfar, ynear, y_sem.at[0], y_sem.at[1])
    ring_z = Ring8(z, at_z(z + 1), at_z(z + 7), lambda i, h: part.at[pl.ds(2 * h, 2), :, i, rows(ZR)],
                   zslot, z_sem.at[0], z_sem.at[1])
    ring_xy = Ring4(y, at_y(y + 1), at_y(y + 3), lambda i, h: part.at[x, i, pl.ds(4 * h, 4), rows(XR)],
                    x2far, x2near, x2_sem.at[0], x2_sem.at[1])
    ring_yx = Ring4(x, at_x(x + 1), at_x(x + 3), lambda i, h: part.at[i, y, pl.ds(4 * h, 4), rows(YR)],
                    y2far, y2near, y2_sem.at[0], y2_sem.at[1])
    ring_zx = Ring4(x, at_x(x + 1), at_x(x + 3), lambda i, h: part.at[i, pl.ds(2 * h, 2), z, rows(ZR)],
                    w2far, w2near, w2_sem.at[0], w2_sem.at[1])
    ring_z.start()
    ring_x.start()
    ring_y.start()
    ring_z.step(2)
    ring_z.step(3)
    ring_x.middle()
    ring_y.middle()
    ring_z.step(4)
    ring_z.step(5)
    ring_z.step(6)
    ring_x.finish()
    ring_xy.start()
    ring_z.finish()
    ring_zx.start()
    ring_y.finish()
    ring_yx.start()
    ring_xy.middle()
    ring_zx.middle()
    ring_yx.middle()
    ring_xy.finish()
    ring_zx.finish()
    ring_yx.finish()
    rest_z = []
    for k in range(1, 8):
        rest_z.append(copy_to(at_z(z + k), part.at[x, y, (z + k) % 8, pl.ds(0, XY)], z3.at[k - 1],
                              z3_sem.at[0, k - 1], z3_sem.at[1, k - 1]))
        rest_z[-1].start()
    rest_y = []
    for k in range(1, 4):
        rest_y.append(copy_to(at_y(y + k), part.at[x, (y + k) % 4, z, rows(ZR)], y3.at[k - 1],
                              y3_sem.at[0, k - 1], y3_sem.at[1, k - 1]))
        rest_y[-1].start()
    total = part[x, y, z, ZR[0]:]
    for k, c in enumerate(rest_y):
        c.wait_recv()
        total = total + y3[k]
    ar[col, ZR[0]:] = total
    total = part[x, y, z, :XY]
    for k, c in enumerate(rest_z):
        c.wait_recv()
        total = total + z3[k]
    ar[col, :XY] = total
    amp_out[...] = ar[col]

    def t1(k):
        return copy_to((row, y * 4 + (zlo + k) % 4), ar.at[col], ar.at[col], t1_sem.at[0, k], t1_sem.at[1, k])

    def t1_from(k):
        there = y * 4 + (zlo + 4 - k) % 4
        return copy_to((row, there), ar.at[there], ar.at[there], t1_sem.at[0, k], t1_sem.at[1, k])

    def t1y(j, k):
        held = y * 4 + (zlo + 4 - j) % 4
        return copy_to(at_y(y + k), ar.at[held], ar.at[held], t1y_sem.at[0, j, k], t1y_sem.at[1, j, k])

    def t1y_from(j, k):
        there = ((y + 4 - k) % 4) * 4 + (zlo + 4 - j) % 4
        return copy_to(at_y(y + k), ar.at[there], ar.at[there], t1y_sem.at[0, j, k], t1y_sem.at[1, j, k])

    half = zlo % 2

    def t2(i):
        device = (((x + i // 2) % 4) * 4 + ((zhi + i % 2) % 2) * 2 + half, row)
        return copy_to(device, ar.at[col], ac.at[col], t2_send.at[i], t2_recv.at[col // 2])

    stay = pltpu.make_async_copy(ar.at[col], ac.at[col], t2_recv.at[col // 2])
    for k in range(1, 4):
        t1(k).start()

    @pl.when(diagonal)
    def _():
        stay.start()

    @pl.when(jnp.logical_not(diagonal))
    def _():
        t2(0).start()

    for k in range(1, 4):
        t1y(0, k).start()
    for i in range(1, 8):
        t2(i).start()
    for j in range(1, 4):
        t1_from(j).wait_recv()
        for k in range(1, 4):
            t1y(j, k).start()

    def t3(s):
        return copy_to(other, ac.at[s], ac.at[s], t3_sem.at[0, s], t3_sem.at[1, s])

    def pass_on(j, carry):
        s = 2 * j + core
        copy_to(other, ac.at[s], ac.at[s], t2_send.at[0], t2_recv.at[j]).wait_recv()
        t3(s).start()
        return carry

    lax.fori_loop(0, 8, pass_on, 0)
    for j in range(4):
        for k in range(1, 4):
            t1y_from(j, k).wait_recv()

    def await_other(j, carry):
        t3(2 * j + 1 - core).wait_recv()
        return carry

    lax.fori_loop(0, 8, await_other, 0)

    r_out[...] = jnp.zeros_like(r_out)

    def pair(i, carry):
        a = jnp.concatenate([ar[2 * i], ar[2 * i + 1]], axis=1)
        b = jnp.concatenate([ac[2 * i], ac[2 * i + 1]], axis=1)
        b_hi = b.astype(jnp.bfloat16)
        b_lo = (b - b_hi.astype(jnp.float32)).astype(jnp.bfloat16)
        both = jnp.concatenate([b_hi, b_lo], axis=0)
        p = pole[:, pl.ds(pl.multiple_of(256 * i, 256), 256)]
        his, los = [], []
        for e in range(8):
            scaled = a * p[e:e + 1]
            hi = scaled.astype(jnp.bfloat16)
            his.append(hi)
            los.append((scaled - hi.astype(jnp.float32)).astype(jnp.bfloat16))
        hi = jnp.concatenate(his, axis=0)
        lo = jnp.concatenate(los, axis=0)
        contract = (((1,), (1,)), ((), ()))
        one = lax.dot_general(hi, both, contract, preferred_element_type=jnp.float32)
        two = lax.dot_general(lo, b_hi, contract, preferred_element_type=jnp.float32)
        r_out[...] += (one[:, :128] + (one[:, 128:] + two)).reshape(8, 128, 128)
        return carry

    lax.fori_loop(0, 8, pair, 0)

    def close_a2a(j, carry):
        a2a(j).wait_send()
        return carry

    lax.fori_loop(1, 16, close_a2a, 0)

    def close_forward(j, carry):
        forward(j).wait_send()
        return carry

    lax.fori_loop(0, 16, close_forward, 0)
    give_s.wait_send()
    for ring in (ring_x, ring_y, ring_z, ring_xy, ring_yx, ring_zx):
        ring.close()
    for c in rest_z + rest_y:
        c.wait_send()
    for k in range(1, 4):
        t1(k).wait_send()
        for j in range(4):
            t1y(j, k).wait_send()

    @pl.when(jnp.logical_not(diagonal))
    def _():
        t2(0).wait_send()

    for i in range(1, 8):
        t2(i).wait_send()

    def close_t3(j, carry):
        t3(2 * j + core).wait_send()
        return carry

    lax.fori_loop(0, 8, close_t3, 0)


def local(surface, eigvec, eig_energy, energies):
    width = surface.shape[1]
    f32, bf16 = jnp.float32, jnp.bfloat16
    dma = pltpu.SemaphoreType.DMA
    nx, ny, nz = XR[1], YR[1], ZR[1]
    vmem = pl.BlockSpec(memory_space=pltpu.VMEM)
    return pl.pallas_call(
        kernel,
        out_shape=(jax.ShapeDtypeStruct((128, 128), f32), jax.ShapeDtypeStruct((8, 128, 128), f32)),
        in_specs=[pl.BlockSpec(memory_space=pl.ANY)] * 2 + [vmem] * 2,
        out_specs=(vmem, vmem),
        scratch_shapes=[
            pltpu.VMEM((2, 8, 128, width), bf16),
            pltpu.VMEM((2, 16, width, 128), bf16),
            pltpu.VMEM((4, 4, 8, 128, 128), f32),
            pltpu.VMEM((2, 4, 4, nx, 128), f32),
            pltpu.VMEM((2, 2, 4, 4, nx, 128), f32),
            pltpu.VMEM((2, 4, 4, ny, 128), f32),
            pltpu.VMEM((2, 2, 4, 4, ny, 128), f32),
            pltpu.VMEM((2, 7, 2, 4, nz, 128), f32),
            pltpu.VMEM((2, 4, nx, 128), f32),
            pltpu.VMEM((2, 2, 4, nx, 128), f32),
            pltpu.VMEM((2, 4, ny, 128), f32),
            pltpu.VMEM((2, 2, 4, ny, 128), f32),
            pltpu.VMEM((2, 2, nz, 128), f32),
            pltpu.VMEM((2, 2, 2, nz, 128), f32),
            pltpu.VMEM((7, XY, 128), f32),
            pltpu.VMEM((3, nz, 128), f32),
            pltpu.VMEM((16, 128, 128), f32),
            pltpu.VMEM((16, 128, 128), f32),
            pltpu.VMEM((8, 2048), f32),
            dma((2,)), dma((2,)), dma((16,)), dma((16,)), dma((16,)), dma((16,)),
            dma((2, 6)), dma((2, 6)), dma((2, 2, 7)), dma((2, 6)), dma((2, 6)), dma((2, 6)),
            dma((2, 7)), dma((2, 3)), dma((2, 4)), dma((2, 4, 4)), dma((8,)), dma((8,)), dma((2, 16)),
        ],
        compiler_params=pltpu.CompilerParams(
            collective_id=0, has_side_effects=True, vmem_limit_bytes=48 * 1024 * 1024
        ),
    )(
        surface.reshape(8, 2, 128, width),
        eigvec.reshape(16, width, 128),
        eig_energy.reshape(1, -1),
        energies.reshape(-1, 1),
    )


def solution(mesh):
    in_specs = (P(None, ("row", "col")), P("row", "col"), P(), P())
    out_specs = (P("row", "col"), P(None, "row", "col"))
    return jax.shard_map(local, mesh=mesh, in_specs=in_specs, out_specs=out_specs, check_vma=False)
```

time: 1660 us -> 145 us (0.09)
  waiting for transfers between devices: 1550 us -> 0 us
  Pallas kernels: 0 us -> 138 us
  blocking collectives: 53.7 us -> 0 us
  matrix products: 31.3 us -> 0 us
    reduce_scatter x1 -> x0, waiting for transfers between devices: 1190 us -> none  [local(): lax.psum_scatter(jnp.dot(surface, rows_all, preferred_element_type=jnp.fl...]
    psum x1 -> x0, waiting for transfers between devices: 188 us -> none  [spread(): return lax.psum(block, axis)]
    all_gather x1 -> x0, waiting for transfers between devices: 179 us -> none  [local(): panel_own = lax.all_gather(sliver, 'col', axis=0, tiled=True)]
    pallas_call x0 -> x1, Pallas kernels: none -> 138 us  [local(): pl.pallas_call(kernel, out_shape=(jax.ShapeDtypeStruct((128, 128), f32),...]
    all_to_all x1 -> x0, blocking collectives: 53.7 us -> none  [local(): lax.all_to_all(eigvec, 'col', split_axis=0, concat_axis=1, tiled=True)]
    dot_general x9 -> x0, matrix products: 31.3 us -> none  [the longest x8 23.1 us: one_energy(): lax.dot_general(scaled, received, (((1,), (1,)), ((), ())), precision=lax...]
  transfers between devices with their start and end apart: 3 -> 0, of which waited for: 3 -> 0; matrix products, arithmetic and copies ran while one was open for 0% -> 0% of each run, Pallas kernels for 0% -> 0%
where the time goes in v1:
time: 145 us
  Pallas kernels  138 us (95%)
  local copies, waits for them, and re-layouts  6.5 us (4%)
    pallas_call x1, Pallas kernels, local(): pl.pallas_call(kernel, out_shape=(jax.ShapeDtypeStruct((128, 128), f32),...  138 us
    unnamed x7, local copies, waits for them, and re-layouts  5.77 us

profile of v1, /device:TPU:7, one launch (start us, length us, event | category | flops | bytes accessed | tf_op | source)
XLA Modules:
  0.0 145.0 jit_solution(18066388911486276728)
XLA Ops:
  0.6 0.7 copy.7.energies
  1.4 0.0 copy-start.1
  1.4 2.8 %copy.6 = bf16[2048,464]{1,0:T(8,128)(2,1)S(1)} copy(bf16[2048,464]{0,1:T(8,128)(2,1)} %param.4) | data formatting | bytes 3801088 | tf_op args[0]
  4.2 0.0 copy-done.1
  4.2 0.0 copy-start
  4.2 1.5 %copy-done = bf16[7424,128]{1,0:T(8,128)(2,1)S(1)} copy-done((bf16[7424,128]{1,0:T(8,128)(2,1)S(1)}, bf16[7424,128]{1,0:T(8,128)(2,1)}, u32[]{:S(2)}) %copy-start) | copy-done | bytes 1900568
  5.7 137.9 %shard_map.59 = (f32[128,128]{1,0:T(8,128)S(1)}, f32[8,128,128]{2,1,0:T(8,128)S(1)}) custom-call(bf16[8,2,128,464]{3,2,1,0:T(8,128)(2,1)S(1)} %bitcast.4, bf16[16,464,128]{2,1,0:T(8,128)(2,1)S(1)} %bitcast.5, f32[1,2048]{1,0:T(1,128)S(1)} %bitcast.6, f32[8,1]{1,0:T(8,128)S(1)} %copy.7.energies), custom_call_target="tpu_custom_call" | custom-call | tf_op jit(solution)/shard_map/pallas_call | solution.py:421
  143.6 0.6 copy.10
  144.2 0.8 copy.11
Async XLA Ops:
  1.4 2.8 %copy-start.1 = (f32[2048]{0:T(1024)S(1)}, f32[2048]{0:T(1024)}, u32[]{:S(2)}) copy-start(f32[2048]{0:T(1024)} %param.6) | copy-start | bytes 24580
  4.2 1.5 %copy-start = (bf16[7424,128]{1,0:T(8,128)(2,1)S(1)}, bf16[7424,128]{1,0:T(8,128)(2,1)}, u32[]{:S(2)}) copy-start(bf16[7424,128]{1,0:T(8,128)(2,1)} %param.5) | copy-start | bytes 5701636

commit v2 on v1

v2 whole, which is shorter than its diff:
```python
import functools
import math

import jax
import jax.numpy as jnp
from jax import lax
from jax.experimental import pallas as pl
from jax.experimental.pallas import tpu as pltpu
from jax.sharding import PartitionSpec as P

MESH = pl.DeviceIdType.MESH
GROUPS = ((32, 24, 8), (32, 16, 16))


def copy_to(device, src, dst, send, recv):
    return pltpu.make_async_remote_copy(
        src_ref=src, dst_ref=dst, send_sem=send, recv_sem=recv, device_id=device, device_id_type=MESH
    )


def add_into(dst, *srcs):
    shape = dst.shape
    if len(shape) == 2:
        total = dst[...]
        for s in srcs:
            total = total + s[...]
        dst[...] = total
        return
    lead = shape[:-2]
    count = math.prod(lead)

    def body(i, carry):
        at = (i,) if len(lead) == 1 else (i // lead[1], i % lead[1])
        total = dst[at]
        for s in srcs:
            total = total + s[at]
        dst[at] = total
        return carry

    lax.fori_loop(0, count, body, 0)


class Ring4:
    def __init__(self, at, plus, minus, chunk, far, near, send, recv):
        self.at, self.chunk, self.near = at, chunk, near
        up, down, across = (at + 1) % 4, (at + 3) % 4, (at + 2) % 4
        self.up, self.down, self.far = up, down, far
        c = functools.partial
        self.p1 = copy_to(plus, chunk(across, 0), far.at[0], send.at[0], recv.at[0])
        self.m1 = copy_to(minus, chunk(across, 1), far.at[1], send.at[1], recv.at[1])
        self.p2 = copy_to(plus, chunk(up, 1), near.at[0, 1], send.at[2], recv.at[2])
        self.m2 = copy_to(minus, chunk(down, 0), near.at[1, 0], send.at[3], recv.at[3])
        self.p3 = copy_to(plus, chunk(up, 0), near.at[0, 0], send.at[4], recv.at[4])
        self.m3 = copy_to(minus, chunk(down, 1), near.at[1, 1], send.at[5], recv.at[5])

    def start(self):
        for c in (self.p1, self.m1, self.p2, self.m2):
            c.start()

    def middle(self):
        self.p1.wait_recv()
        add_into(self.chunk(self.up, 0), self.far.at[0])
        self.p3.start()
        self.m1.wait_recv()
        add_into(self.chunk(self.down, 1), self.far.at[1])
        self.m3.start()

    def finish(self):
        for c in (self.p2, self.m2, self.p3, self.m3):
            c.wait_recv()
        for h in range(2):
            add_into(self.chunk(self.at, h), self.near.at[0, h], self.near.at[1, h])

    def close(self):
        for c in (self.p1, self.m1, self.p2, self.m2, self.p3, self.m3):
            c.wait_send()


class Ring8:
    def __init__(self, at, plus, minus, chunk, slots, send, recv):
        self.at, self.chunk, self.slots = at, chunk, slots
        self.copies, self.held = [], []
        for s in range(7):
            k = 4 - (s + 1) // 2
            h = 0 if s % 2 == 0 else 1
            pair, held = [], []
            for way, device in ((0, plus), (1, minus)):
                i = (at + k) % 8 if way == 0 else (at + 8 - k) % 8
                half = h if way == 0 else 1 - h
                view = chunk(i, half)
                held.append(view)
                pair.append(copy_to(device, view, slots.at[way, s], send.at[way, s], recv.at[way, s]))
            self.copies.append(pair)
            self.held.append(held)

    def start(self):
        for s in range(2):
            for c in self.copies[s]:
                c.start()

    def step(self, s):
        for way in range(2):
            self.copies[s - 2][way].wait_recv()
            add_into(self.held[s][way], self.slots.at[way, s - 2])
            self.copies[s][way].start()

    def finish(self):
        for s in (5, 6):
            for way in range(2):
                self.copies[s][way].wait_recv()
        add_into(self.chunk(self.at, 0), self.slots.at[0, 6], self.slots.at[1, 5])
        add_into(self.chunk(self.at, 1), self.slots.at[0, 5], self.slots.at[1, 6])

    def close(self):
        for pair in self.copies:
            for c in pair:
                c.wait_send()


class Group:
    def __init__(self, where, part, ar, ac, first, sizes, buf, sem):
        (row, col, x, y, zhi, zlo, core), (at_x, at_y, at_z, other) = where
        z = zhi * 4 + zlo
        nx, ny, nz = sizes
        xr, yr, zr = pl.ds(first, nx), pl.ds(first + nx, ny), pl.ds(first + nx + ny, nz)
        self.xy, self.zr, self.all = pl.ds(first, nx + ny), zr, pl.ds(first, nx + ny + nz)
        self.where, self.part, self.ar, self.ac, self.sem, self.buf = where, part, ar, ac, sem, buf
        xp, xm, yp, ym, zp, zm = at_x(x + 1), at_x(x + 3), at_y(y + 1), at_y(y + 3), at_z(z + 1), at_z(z + 7)
        quarter = lambda h: pl.ds(2 * h, 2)
        ring = lambda k, i, plus, minus, chunk: Ring4(i, plus, minus, chunk, buf[2 * k], buf[2 * k + 1], sem[k].at[0], sem[k].at[1])
        near, far = pl.ds(zlo // 2 * 2, 2), pl.ds(2 - zlo // 2 * 2, 2)
        self.x1n = ring(0, x, xp, xm, lambda i, h: part.at[i, :, h, near, xr])
        self.x1f = ring(1, x, xp, xm, lambda i, h: part.at[i, :, h, far, xr])
        self.y1n = ring(2, y, yp, ym, lambda i, h: part.at[:, i, h, near, yr])
        self.y1f = ring(3, y, yp, ym, lambda i, h: part.at[:, i, h, far, yr])
        self.x2n = ring(4, y, yp, ym, lambda i, h: part.at[x, i, h, near, xr])
        self.x2f = ring(5, y, yp, ym, lambda i, h: part.at[x, i, h, far, xr])
        self.y2n = ring(6, x, xp, xm, lambda i, h: part.at[i, y, h, near, yr])
        self.y2f = ring(7, x, xp, xm, lambda i, h: part.at[i, y, h, far, yr])
        self.z2 = ring(8, x, xp, xm, lambda i, h: part.at[i, quarter(h), zhi, zlo, zr])
        self.z1 = Ring8(z, zp, zm, lambda i, h: part.at[quarter(h), :, i // 4, i % 4, zr], buf[18], sem[9].at[0], sem[9].at[1])
        self.last_z = [
            copy_to(at_z(z + k), part.at[x, y, (z + k) % 8 // 4, (z + k) % 4, self.xy], buf[19].at[k - 1], sem[10].at[0, k], sem[10].at[1, k])
            for k in range(1, 8)
        ]
        self.last_y = [
            copy_to(at_y(y + k), part.at[x, (y + k) % 4, zhi, zlo, zr], buf[20].at[k - 1], sem[11].at[0, k], sem[11].at[1, k])
            for k in range(1, 4)
        ]

    def finish_sums(self):
        (row, col, x, y, zhi, zlo, core), _ = self.where
        for rows, copies, slots in ((self.zr, self.last_y, self.buf[20]), (self.xy, self.last_z, self.buf[19])):
            total = self.part[x, y, zhi, zlo, rows]
            for k, c in enumerate(copies):
                c.wait_recv()
                total = total + slots[k]
            self.ar[col, rows] = total

    def near(self, there, device, k):
        view = self.ar.at[there, self.all]
        return copy_to(device, view, view, self.sem[12].at[0, k], self.sem[12].at[1, k])

    def near_send(self, k):
        (row, col, x, y, zhi, zlo, core), _ = self.where
        return self.near(col, (row, y * 4 + (zlo + k) % 4), k)

    def near_recv(self, k):
        (row, col, x, y, zhi, zlo, core), _ = self.where
        there = y * 4 + (zlo + 4 - k) % 4
        return self.near(there, (row, there), k)

    def along_y(self, there, j, k):
        (row, col, x, y, zhi, zlo, core), (at_x, at_y, at_z, other) = self.where
        view = self.ar.at[there, self.all]
        return copy_to(at_y(y + k), view, view, self.sem[13].at[0, j, k], self.sem[13].at[1, j, k])

    def along_y_send(self, j, k):
        (row, col, x, y, zhi, zlo, core), _ = self.where
        return self.along_y(y * 4 + (zlo + 4 - j) % 4, j, k)

    def along_y_recv(self, j, k):
        (row, col, x, y, zhi, zlo, core), _ = self.where
        return self.along_y(((y + 4 - k) % 4) * 4 + (zlo + 4 - j) % 4, j, k)

    def across(self, i):
        (row, col, x, y, zhi, zlo, core), _ = self.where
        device = (((x + i // 2) % 4) * 4 + ((zhi + i % 2) % 2) * 2 + zlo % 2, row)
        return copy_to(device, self.ar.at[col, self.all], self.ac.at[col, self.all], self.sem[14].at[i], self.sem[15].at[col // 2])

    def stay(self):
        (row, col, x, y, zhi, zlo, core), _ = self.where
        return pltpu.make_async_copy(self.ar.at[col, self.all], self.ac.at[col, self.all], self.sem[15].at[col // 2])

    def hand(self, s):
        (row, col, x, y, zhi, zlo, core), (at_x, at_y, at_z, other) = self.where
        view = self.ac.at[s, self.all]
        return copy_to(other, view, view, self.sem[16].at[0, s], self.sem[16].at[1, s])

    def start_gather(self):
        (row, col, x, y, zhi, zlo, core), _ = self.where
        for k in range(1, 4):
            self.near_send(k).start()

        @pl.when(row == col)
        def _():
            self.stay().start()

        @pl.when(row != col)
        def _():
            self.across(0).start()

        for k in range(1, 4):
            self.along_y_send(0, k).start()
        for i in range(1, 8):
            self.across(i).start()

    def middle_gather(self):
        for j in range(1, 4):
            self.near_recv(j).wait_recv()
            for k in range(1, 4):
                self.along_y_send(j, k).start()

    def pass_on(self):
        (row, col, x, y, zhi, zlo, core), (at_x, at_y, at_z, other) = self.where

        def body(j, carry):
            s = 2 * j + core
            view = self.ac.at[s, self.all]
            copy_to(other, view, view, self.sem[14].at[0], self.sem[15].at[j]).wait_recv()
            self.hand(s).start()
            return carry

        lax.fori_loop(0, 8, body, 0)

    def finish_gather(self):
        (row, col, x, y, zhi, zlo, core), _ = self.where
        for j in range(4):
            for k in range(1, 4):
                self.along_y_recv(j, k).wait_recv()

        def body(j, carry):
            self.hand(2 * j + 1 - core).wait_recv()
            return carry

        lax.fori_loop(0, 8, body, 0)

    def close_sums(self):
        for ring in (self.x1n, self.x1f, self.y1n, self.y1f, self.z1, self.x2n, self.x2f, self.y2n, self.y2f, self.z2):
            ring.close()
        for c in self.last_z + self.last_y:
            c.wait_send()

    def close_gather(self):
        (row, col, x, y, zhi, zlo, core), _ = self.where
        for k in range(1, 4):
            self.near_send(k).wait_send()
            for j in range(4):
                self.along_y_send(j, k).wait_send()

        @pl.when(row != col)
        def _():
            self.across(0).wait_send()

        for i in range(1, 8):
            self.across(i).wait_send()

        def body(j, carry):
            self.hand(2 * j + core).wait_send()
            return carry

        lax.fori_loop(0, 8, body, 0)


def group_buffers(sizes):
    nx, ny, nz = sizes
    one = lambda *lead: [(2,) + lead, (2, 2) + lead]
    shapes = one(4, 2, nx) * 2 + one(4, 2, ny) * 2 + one(2, nx) * 2 + one(2, ny) * 2 + one(2, nz)
    shapes += [(2, 7, 2, 4, nz), (7, nx + ny), (3, nz)]
    return [pltpu.VMEM(s + (128,), jnp.float32) for s in shapes]


def group_sems():
    shapes = [(2, 6)] * 9 + [(2, 2, 7), (2, 8), (2, 4), (2, 4), (2, 4, 4), (8,), (8,), (2, 16)]
    return [pltpu.SemaphoreType.DMA(s) for s in shapes]


def kernel(
    surf, eig, levels_in, energies_in, amp_out, r_out, s_raw, s_buf, v_buf, part, ar, ac, pole, levels, energies,
    loc_sem, s_send, s_recv, a_send, a_recv, f_send, f_recv, *rest,
):
    row, col = lax.axis_index("row"), lax.axis_index("col")
    x, zhi, core = row // 4, (row // 2) % 2, row % 2
    y, zlo = col // 4, col % 4
    z = zhi * 4 + zlo
    other = (row + 1 - 2 * core, col)

    def at_x(i):
        return ((i % 4) * 4 + zhi * 2 + core, col)

    def at_y(i):
        return (row, (i % 4) * 4 + zlo)

    def at_z(i):
        i = i % 8
        return (x * 4 + (i // 4) * 2 + core, y * 4 + i % 4)

    def load_s(i):
        return pltpu.make_async_copy(surf.at[:, columns(2 * i + core)], s_raw.at[0, i], loc_sem.at[i])

    def give_s(i):
        return copy_to(other, surf.at[:, columns(2 * i + 1 - core)], s_raw.at[1, i], s_send.at[i], s_recv.at[i])

    def columns(i):
        return pl.ds(pl.multiple_of(128 * i, 128), 128)

    for i in range(8):
        load_s(i).start()
    load_levels = pltpu.make_async_copy(levels_in, levels, loc_sem.at[9])
    load_levels.start()
    load_energies = pltpu.make_async_copy(energies_in, energies, loc_sem.at[10])
    load_energies.start()
    load_v = pltpu.make_async_copy(eig.at[col], v_buf.at[0, 0], loc_sem.at[8])
    load_v.start()

    barrier = pltpu.get_barrier_semaphore()

    def greet(device):
        pl.semaphore_signal(barrier, inc=1, device_id=device, device_id_type=MESH)

    def greet_col(j, carry):
        greet((row, ((y + j // 4) % 4) * 4 + (zlo + j % 4) % 4))
        return carry

    lax.fori_loop(1, 16, greet_col, 0)
    greet(other)
    greet(at_x(x + 1))
    greet(at_x(x + 3))

    def greet_z(j, carry):
        greet((x * 4 + (1 - zhi) * 2 + core, y * 4 + j))
        return carry

    lax.fori_loop(0, 4, greet_z, 0)

    def greet_t2(j, carry):
        source = 2 * j + core

        @pl.when(jnp.logical_or(row != col, source != col))
        def _():
            greet((col, source))

        return carry

    lax.fori_loop(0, 8, greet_t2, 0)
    diagonal = row == col
    pl.semaphore_wait(barrier, jnp.where(diagonal, 29, 30))

    def a2a(j):
        dest = ((y + j % 4) % 4) * 4 + apart(j // 4)
        return copy_to((row, dest), eig.at[dest], v_buf.at[0, j], a_send.at[j], a_recv.at[j])

    def apart(k):
        low, high = (zlo + k) % 2, (zlo // 2 + k // 2) % 2
        return high * 2 + low

    def send_a2a(i, carry):
        a2a((i + 7) % 15 + 1).start()
        return carry

    lax.fori_loop(0, 15, send_a2a, 0)
    for i in range(8):
        give_s(i).start()
    load_levels.wait()
    load_energies.wait()
    for e in range(8):
        pole[e:e + 1] = (1.0 / math.sqrt(2048.0)) / (levels[...] - energies[e])

    def forward(j):
        return copy_to(other, v_buf.at[0, j], v_buf.at[1, j], f_send.at[j], f_recv.at[j])

    load_v.wait()
    forward(0).start()
    for i in range(8):
        load_s(i).wait()
        s_buf[0, 128 * i:128 * i + 128] = s_raw[0, i].T
    for i in range(8):
        give_s(i).wait_recv()
        s_buf[1, 128 * i:128 * i + 128] = s_raw[1, i].T

    def multiply(i):
        zs = apart(i // 2)
        got = None
        for q in range(2):
            two = jnp.concatenate([v_buf[q, 2 * i], v_buf[q, 2 * i + 1]], axis=1)
            one = jnp.dot(s_buf[q], two, preferred_element_type=jnp.float32)
            got = one if got is None else got + one
        for h in range(2):
            ys = (y + 4 - (2 * i + h) % 4) % 4
            for xi in range(4):
                for zh in range(2):
                    at = (xi * 2 + zh) * 128
                    part[xi, ys, zh, zs] = got[at:at + 128, h * 128:h * 128 + 128]

    def take(j):
        a2a(j).wait_recv()
        forward(j).start()

    where = (row, col, x, y, zhi, zlo, core), (at_x, at_y, at_z, other)
    groups, first, per = [], 0, len(rest) // len(GROUPS)
    for g, sizes in enumerate(GROUPS):
        own = rest[g * per:(g + 1) * per]
        groups.append(Group(where, part, ar, ac, first, sizes, own[:21], own[21:]))
        first += sum(sizes)
    def step(i, carry):
        take(2 * i)
        take(2 * i + 1)
        forward(2 * i - 2).wait_recv()
        forward(2 * i - 1).wait_recv()
        multiply(i - 1)
        return carry

    def drain(i):
        forward(2 * i).wait_recv()
        forward(2 * i + 1).wait_recv()
        multiply(i)

    take(1)
    lax.fori_loop(1, 4, step, 0)
    drain(3)
    a, b = groups
    a.x1n.start()
    a.y1n.start()
    a.x1n.middle()
    b.x1n.start()
    a.y1n.middle()
    b.y1n.start()
    a.x1n.finish()
    a.x2n.start()
    take(8)
    take(9)
    lax.fori_loop(5, 7, step, 0)
    b.x1n.middle()
    a.y1n.finish()
    a.y2n.start()
    b.y1n.middle()
    b.x1n.finish()
    a.y2n.middle()
    b.x2n.start()
    a.x2n.middle()
    lax.fori_loop(7, 8, step, 0)
    drain(7)
    a.x1f.start()
    a.y1f.start()
    a.z1.start()
    a.y2n.finish()
    b.y1n.finish()
    b.y2n.start()
    b.x2n.middle()
    a.z1.step(2)
    a.z1.step(3)
    a.x1f.middle()
    b.x1f.start()
    a.x2n.finish()
    a.z1.step(4)
    a.z1.step(5)
    b.z1.start()
    a.y1f.middle()
    b.y2n.middle()
    b.y1f.start()
    a.z1.step(6)
    b.x2n.finish()
    a.x1f.finish()
    a.x2f.start()
    b.z1.step(2)
    a.y1f.finish()
    a.y2f.start()
    b.z1.step(3)
    b.x1f.middle()
    b.y1f.middle()
    a.z1.finish()
    a.z2.start()
    a.x2f.middle()
    b.z1.step(4)
    b.y2n.finish()
    a.y2f.middle()
    b.z1.step(5)
    b.y1f.finish()
    b.y2f.start()
    a.x2f.finish()
    b.z1.step(6)
    b.x1f.finish()
    a.z2.middle()
    b.x2f.start()
    a.y2f.finish()
    for copy in a.last_z:
        copy.start()
    b.y2f.middle()
    a.z2.finish()
    for copy in a.last_y:
        copy.start()
    b.x2f.middle()
    b.y2f.finish()
    b.z1.finish()
    b.z2.start()
    b.x2f.finish()
    b.z2.middle()
    for copy in b.last_z:
        copy.start()
    b.z2.finish()
    for copy in b.last_y:
        copy.start()
    a.finish_sums()
    a.start_gather()
    b.finish_sums()
    b.start_gather()
    a.middle_gather()
    a.pass_on()
    b.middle_gather()
    a.finish_gather()
    b.pass_on()
    b.finish_gather()
    amp_out[...] = ar[col]


    r_out[...] = jnp.zeros_like(r_out)

    def pair(i, carry):
        a = jnp.concatenate([ar[2 * i], ar[2 * i + 1]], axis=1)
        b = jnp.concatenate([ac[2 * i], ac[2 * i + 1]], axis=1)
        b_hi = b.astype(jnp.bfloat16)
        b_lo = (b - b_hi.astype(jnp.float32)).astype(jnp.bfloat16)
        both = jnp.concatenate([b_hi, b_lo], axis=0)
        p = pole[:, pl.ds(pl.multiple_of(256 * i, 256), 256)]
        his, los = [], []
        for e in range(8):
            scaled = a * p[e:e + 1]
            hi = scaled.astype(jnp.bfloat16)
            his.append(hi)
            los.append((scaled - hi.astype(jnp.float32)).astype(jnp.bfloat16))
        hi = jnp.concatenate(his, axis=0)
        lo = jnp.concatenate(los, axis=0)
        contract = (((1,), (1,)), ((), ()))
        one = lax.dot_general(hi, both, contract, preferred_element_type=jnp.float32)
        two = lax.dot_general(lo, b_hi, contract, preferred_element_type=jnp.float32)
        r_out[...] += (one[:, :128] + (one[:, 128:] + two)).reshape(8, 128, 128)
        return carry

    lax.fori_loop(0, 8, pair, 0)

    def close_a2a(j, carry):
        a2a(j).wait_send()
        return carry

    lax.fori_loop(1, 16, close_a2a, 0)

    def close_forward(j, carry):
        forward(j).wait_send()
        return carry

    lax.fori_loop(0, 16, close_forward, 0)
    for i in range(8):
        give_s(i).wait_send()
    for g in groups:
        g.close_sums()
        g.close_gather()


def local(surface, eigvec, eig_energy, energies):
    width = surface.shape[1]
    f32, bf16 = jnp.float32, jnp.bfloat16
    dma = pltpu.SemaphoreType.DMA
    vmem = pl.BlockSpec(memory_space=pltpu.VMEM)
    return pl.pallas_call(
        kernel,
        out_shape=(jax.ShapeDtypeStruct((128, 128), f32), jax.ShapeDtypeStruct((8, 128, 128), f32)),
        in_specs=[pl.BlockSpec(memory_space=pl.ANY)] * 4,
        out_specs=(vmem, vmem),
        scratch_shapes=[
            pltpu.VMEM((2, 8, width, 128), bf16),
            pltpu.VMEM((2, 1024, width), bf16),
            pltpu.VMEM((2, 16, width, 128), bf16),
            pltpu.VMEM((4, 4, 2, 4, 128, 128), f32),
            pltpu.VMEM((16, 128, 128), f32),
            pltpu.VMEM((16, 128, 128), f32),
            pltpu.VMEM((8, 2048), f32),
            pltpu.VMEM((1, 2048), f32),
            pltpu.SMEM((8,), f32),
            dma((11,)), dma((8,)), dma((8,)), dma((16,)), dma((16,)), dma((16,)), dma((16,)),
        ] + [item for sizes in GROUPS for item in group_buffers(sizes) + group_sems()],
        compiler_params=pltpu.CompilerParams(
            collective_id=0, has_side_effects=True, vmem_limit_bytes=60 * 1024 * 1024
        ),
    )(
        surface.T,
        eigvec.reshape(16, width, 128),
        eig_energy.reshape(1, -1),
        energies,
    )


def solution(mesh):
    in_specs = (P(None, ("row", "col")), P("row", "col"), P(), P())
    out_specs = (P("row", "col"), P(None, "row", "col"))
    return jax.shard_map(local, mesh=mesh, in_specs=in_specs, out_specs=out_specs, check_vma=False)
```

time: 145 us -> 140 us (0.966)
  local copies, waits for them, and re-layouts: 6.5 us -> 3.34 us
  Pallas kernels: 138 us -> 135 us
    pallas_call x1, Pallas kernels: 138 us -> 135 us  [local(): pl.pallas_call(kernel, out_shape=(jax.ShapeDtypeStruct((128, 128), f32),...]
    unnamed x7 -> x2, local copies, waits for them, and re-layouts: 5.77 us -> 3.34 us
where the time goes in v2:
time: 140 us; the launch traced here: 139 us
  Pallas kernels  135 us (96%)
  local copies, waits for them, and re-layouts  3.34 us (2%)
    pallas_call x1, Pallas kernels, local(): pl.pallas_call(kernel, out_shape=(jax.ShapeDtypeStruct((128, 128), f32),...  135 us
    unnamed x2, local copies, waits for them, and re-layouts  3.34 us

profile of v2, /device:TPU:7, one launch (start us, length us, event | category | flops | bytes accessed | tf_op | source)
XLA Modules:
  0.0 139.1 jit_solution(6170623849576468899)
XLA Ops:
  0.6 135.1 %shard_map.59 = (f32[128,128]{1,0:T(8,128)}, f32[8,128,128]{2,1,0:T(8,128)}) custom-call(bf16[464,2048]{1,0:T(8,128)(2,1)} %bitcast.3, bf16[16,464,128]{2,1,0:T(8,128)(2,1)} %bitcast.4, f32[1,2048]{1,0:T(1,128)} %bitcast.5, f32[8]{0:T(128)} %energies_in.1), custom_call_target="tpu_custom_call" | custom-call | tf_op jit(solution)/shard_map/pallas_call | solution.py:574
  135.8 1.5 %copy.8 = f32[128,128]{1,0:T(8,128)} copy(f32[128,128]{1,0:T(8,128)} %get-tuple-element.4) | data formatting | bytes 131072
  137.3 1.9 %copy.9 = f32[8,128,128]{2,1,0:T(8,128)} copy(f32[8,128,128]{2,1,0:T(8,128)} %get-tuple-element.5) | data formatting | bytes 1048576

commit v3 on v2

--- a/solution.py
+++ b/solution.py
@@ -9,7 +9,7 @@
 from jax.sharding import PartitionSpec as P
 
 MESH = pl.DeviceIdType.MESH
-GROUPS = ((32, 24, 8), (32, 16, 16))
+GROUPS = ((56, 48, 24),)
 
 
 def copy_to(device, src, dst, send, recv):
@@ -139,14 +139,26 @@
         self.y2f = ring(7, x, xp, xm, lambda i, h: part.at[i, y, h, far, yr])
         self.z2 = ring(8, x, xp, xm, lambda i, h: part.at[i, quarter(h), zhi, zlo, zr])
         self.z1 = Ring8(z, zp, zm, lambda i, h: part.at[quarter(h), :, i // 4, i % 4, zr], buf[18], sem[9].at[0], sem[9].at[1])
-        self.last_z = [
-            copy_to(at_z(z + k), part.at[x, y, (z + k) % 8 // 4, (z + k) % 4, self.xy], buf[19].at[k - 1], sem[10].at[0, k], sem[10].at[1, k])
-            for k in range(1, 8)
-        ]
+        self.last_z = []
+        for k in range(1, 8):
+            high, low = (zhi + k // 4) % 2, ((zlo // 2 + k // 2) % 2) * 2 + (zlo + k) % 2
+            self.last_z.append(copy_to(
+                (x * 4 + high * 2 + core, y * 4 + low), part.at[x, y, high, low, self.xy], buf[19].at[k - 1],
+                sem[10].at[0, k], sem[10].at[1, k],
+            ))
         self.last_y = [
             copy_to(at_y(y + k), part.at[x, (y + k) % 4, zhi, zlo, zr], buf[20].at[k - 1], sem[11].at[0, k], sem[11].at[1, k])
             for k in range(1, 4)
         ]
+
+    def start_last_z(self, near):
+        for k in range(1, 8):
+            if (k in (1, 4, 5)) == near:
+                self.last_z[k - 1].start()
+
+    def start_last_y(self):
+        for c in self.last_y:
+            c.start()
 
     def finish_sums(self):
         (row, col, x, y, zhi, zlo, core), _ = self.where
@@ -286,7 +298,7 @@
 
 
 def kernel(
-    surf, eig, levels_in, energies_in, amp_out, r_out, s_raw, s_buf, v_buf, part, ar, ac, pole, levels, energies,
+    surf, eig, poles, amp_out, r_out, s_raw, s_buf, v_buf, part, ar, ac,
     loc_sem, s_send, s_recv, a_send, a_recv, f_send, f_recv, *rest,
 ):
     row, col = lax.axis_index("row"), lax.axis_index("col")
@@ -316,10 +328,6 @@
 
     for i in range(8):
         load_s(i).start()
-    load_levels = pltpu.make_async_copy(levels_in, levels, loc_sem.at[9])
-    load_levels.start()
-    load_energies = pltpu.make_async_copy(energies_in, energies, loc_sem.at[10])
-    load_energies.start()
     load_v = pltpu.make_async_copy(eig.at[col], v_buf.at[0, 0], loc_sem.at[8])
     load_v.start()
 
@@ -337,24 +345,9 @@
     greet(at_x(x + 1))
     greet(at_x(x + 3))
 
-    def greet_z(j, carry):
-        greet((x * 4 + (1 - zhi) * 2 + core, y * 4 + j))
-        return carry
-
-    lax.fori_loop(0, 4, greet_z, 0)
-
-    def greet_t2(j, carry):
-        source = 2 * j + core
-
-        @pl.when(jnp.logical_or(row != col, source != col))
-        def _():
-            greet((col, source))
-
-        return carry
-
-    lax.fori_loop(0, 8, greet_t2, 0)
-    diagonal = row == col
-    pl.semaphore_wait(barrier, jnp.where(diagonal, 29, 30))
+    greet(at_z(z + 1))
+    greet(at_z(z + 7))
+    pl.semaphore_wait(barrier, 20)
 
     def a2a(j):
         dest = ((y + j % 4) % 4) * 4 + apart(j // 4)
@@ -365,17 +358,12 @@
         return high * 2 + low
 
     def send_a2a(i, carry):
-        a2a((i + 7) % 15 + 1).start()
+        a2a(i + 1).start()
         return carry
 
     lax.fori_loop(0, 15, send_a2a, 0)
     for i in range(8):
         give_s(i).start()
-    load_levels.wait()
-    load_energies.wait()
-    for e in range(8):
-        pole[e:e + 1] = (1.0 / math.sqrt(2048.0)) / (levels[...] - energies[e])
-
     def forward(j):
         return copy_to(other, v_buf.at[0, j], v_buf.at[1, j], f_send.at[j], f_recv.at[j])
 
@@ -428,98 +416,54 @@
     take(1)
     lax.fori_loop(1, 4, step, 0)
     drain(3)
-    a, b = groups
+    a, = groups
     a.x1n.start()
     a.y1n.start()
     a.x1n.middle()
-    b.x1n.start()
     a.y1n.middle()
-    b.y1n.start()
-    a.x1n.finish()
-    a.x2n.start()
     take(8)
     take(9)
     lax.fori_loop(5, 7, step, 0)
-    b.x1n.middle()
-    a.y1n.finish()
-    a.y2n.start()
-    b.y1n.middle()
-    b.x1n.finish()
-    a.y2n.middle()
-    b.x2n.start()
-    a.x2n.middle()
+    a.x1n.finish()
+    a.x2n.start()
     lax.fori_loop(7, 8, step, 0)
     drain(7)
     a.x1f.start()
     a.y1f.start()
     a.z1.start()
-    a.y2n.finish()
-    b.y1n.finish()
-    b.y2n.start()
-    b.x2n.middle()
+    a.y1n.finish()
+    a.y2n.start()
     a.z1.step(2)
+    a.x2n.middle()
     a.z1.step(3)
     a.x1f.middle()
-    b.x1f.start()
-    a.x2n.finish()
     a.z1.step(4)
     a.z1.step(5)
-    b.z1.start()
     a.y1f.middle()
-    b.y2n.middle()
-    b.y1f.start()
+    a.y2n.middle()
     a.z1.step(6)
-    b.x2n.finish()
+    a.x2n.finish()
     a.x1f.finish()
+    a.z1.finish()
+    a.y2n.finish()
     a.x2f.start()
-    b.z1.step(2)
+    a.z2.start()
+    a.start_last_z(True)
     a.y1f.finish()
     a.y2f.start()
-    b.z1.step(3)
-    b.x1f.middle()
-    b.y1f.middle()
-    a.z1.finish()
-    a.z2.start()
+    a.z2.middle()
     a.x2f.middle()
-    b.z1.step(4)
-    b.y2n.finish()
     a.y2f.middle()
-    b.z1.step(5)
-    b.y1f.finish()
-    b.y2f.start()
+    a.z2.finish()
     a.x2f.finish()
-    b.z1.step(6)
-    b.x1f.finish()
-    a.z2.middle()
-    b.x2f.start()
+    a.start_last_y()
     a.y2f.finish()
-    for copy in a.last_z:
-        copy.start()
-    b.y2f.middle()
-    a.z2.finish()
-    for copy in a.last_y:
-        copy.start()
-    b.x2f.middle()
-    b.y2f.finish()
-    b.z1.finish()
-    b.z2.start()
-    b.x2f.finish()
-    b.z2.middle()
-    for copy in b.last_z:
-        copy.start()
-    b.z2.finish()
-    for copy in b.last_y:
-        copy.start()
+    a.start_last_z(False)
     a.finish_sums()
     a.start_gather()
-    b.finish_sums()
-    b.start_gather()
     a.middle_gather()
     a.pass_on()
-    b.middle_gather()
     a.finish_gather()
-    b.pass_on()
-    b.finish_gather()
     amp_out[...] = ar[col]
 
 
@@ -531,7 +475,7 @@
         b_hi = b.astype(jnp.bfloat16)
         b_lo = (b - b_hi.astype(jnp.float32)).astype(jnp.bfloat16)
         both = jnp.concatenate([b_hi, b_lo], axis=0)
-        p = pole[:, pl.ds(pl.multiple_of(256 * i, 256), 256)]
+        p = poles[:, pl.ds(pl.multiple_of(256 * i, 256), 256)]
         his, los = [], []
         for e in range(8):
             scaled = a * p[e:e + 1]
@@ -574,7 +518,7 @@
     return pl.pallas_call(
         kernel,
         out_shape=(jax.ShapeDtypeStruct((128, 128), f32), jax.ShapeDtypeStruct((8, 128, 128), f32)),
-        in_specs=[pl.BlockSpec(memory_space=pl.ANY)] * 4,
+        in_specs=[pl.BlockSpec(memory_space=pl.ANY)] * 2 + [vmem],
         out_specs=(vmem, vmem),
         scratch_shapes=[
             pltpu.VMEM((2, 8, width, 128), bf16),
@@ -583,19 +527,15 @@
             pltpu.VMEM((4, 4, 2, 4, 128, 128), f32),
             pltpu.VMEM((16, 128, 128), f32),
             pltpu.VMEM((16, 128, 128), f32),
-            pltpu.VMEM((8, 2048), f32),
-            pltpu.VMEM((1, 2048), f32),
-            pltpu.SMEM((8,), f32),
-            dma((11,)), dma((8,)), dma((8,)), dma((16,)), dma((16,)), dma((16,)), dma((16,)),
+            dma((9,)), dma((8,)), dma((8,)), dma((16,)), dma((16,)), dma((16,)), dma((16,)),
         ] + [item for sizes in GROUPS for item in group_buffers(sizes) + group_sems()],
         compiler_params=pltpu.CompilerParams(
-            collective_id=0, has_side_effects=True, vmem_limit_bytes=60 * 1024 * 1024
+            collective_id=0, has_side_effects=True, vmem_limit_bytes=52 * 1024 * 1024
         ),
     )(
         surface.T,
         eigvec.reshape(16, width, 128),
-        eig_energy.reshape(1, -1),
-        energies,
+        (1.0 / math.sqrt(2048.0)) / (eig_energy[None, :] - energies[:, None]),
     )
 
 

time: 140 us -> 121 us (0.86)
  Pallas kernels: 135 us -> 117 us
  local copies, waits for them, and re-layouts: 3.34 us -> 1.42 us
    pallas_call x1, Pallas kernels: 135 us -> 117 us  [local(): pl.pallas_call(kernel, out_shape=(jax.ShapeDtypeStruct((128, 128), f32),...]
    unnamed x2, local copies, waits for them, and re-layouts: 3.34 us -> 1.42 us
where the time goes in v3:
time: 121 us; the launch traced here: 120 us
  Pallas kernels  117 us (97%)
  local copies, waits for them, and re-layouts  1.42 us (1%)
    pallas_call x1, Pallas kernels, local(): pl.pallas_call(kernel, out_shape=(jax.ShapeDtypeStruct((128, 128), f32),...  117 us

profile of v3, /device:TPU:7, one launch (start us, length us, event | category | flops | bytes accessed | tf_op | source)
XLA Modules:
  0.0 120.0 jit_solution(5597695836442269442)
XLA Ops:
  0.6 0.8 subtract_divide_fusion.poles
  1.4 117.1 %shard_map.59 = (f32[128,128]{1,0:T(8,128)S(1)}, f32[8,128,128]{2,1,0:T(8,128)S(1)}) custom-call(bf16[464,2048]{1,0:T(8,128)(2,1)} %bitcast.2, bf16[16,464,128]{2,1,0:T(8,128)(2,1)} %bitcast.3, f32[8,2048]{1,0:T(8,128)S(1)} %subtract_divide_fusion.poles), custom_call_target="tpu_custom_call" | custom-call | tf_op jit(solution)/shard_map/pallas_call | solution.py:518
  118.5 0.6 copy.8
  119.2 0.8 copy.9

commit v4 on v3

--- a/solution.py
+++ b/solution.py
@@ -128,33 +128,41 @@
         xp, xm, yp, ym, zp, zm = at_x(x + 1), at_x(x + 3), at_y(y + 1), at_y(y + 3), at_z(z + 1), at_z(z + 7)
         quarter = lambda h: pl.ds(2 * h, 2)
         ring = lambda k, i, plus, minus, chunk: Ring4(i, plus, minus, chunk, buf[2 * k], buf[2 * k + 1], sem[k].at[0], sem[k].at[1])
-        near, far = pl.ds(zlo // 2 * 2, 2), pl.ds(2 - zlo // 2 * 2, 2)
+        near = pl.ds(zlo // 2 * 2, 2)
+        mid, far = (zlo + 2) % 4, (zlo // 2 + 1) % 2 * 2 + (zlo + 1) % 2
         self.x1n = ring(0, x, xp, xm, lambda i, h: part.at[i, :, h, near, xr])
-        self.x1f = ring(1, x, xp, xm, lambda i, h: part.at[i, :, h, far, xr])
-        self.y1n = ring(2, y, yp, ym, lambda i, h: part.at[:, i, h, near, yr])
-        self.y1f = ring(3, y, yp, ym, lambda i, h: part.at[:, i, h, far, yr])
-        self.x2n = ring(4, y, yp, ym, lambda i, h: part.at[x, i, h, near, xr])
-        self.x2f = ring(5, y, yp, ym, lambda i, h: part.at[x, i, h, far, xr])
-        self.y2n = ring(6, x, xp, xm, lambda i, h: part.at[i, y, h, near, yr])
-        self.y2f = ring(7, x, xp, xm, lambda i, h: part.at[i, y, h, far, yr])
-        self.z2 = ring(8, x, xp, xm, lambda i, h: part.at[i, quarter(h), zhi, zlo, zr])
-        self.z1 = Ring8(z, zp, zm, lambda i, h: part.at[quarter(h), :, i // 4, i % 4, zr], buf[18], sem[9].at[0], sem[9].at[1])
+        self.x1m = ring(1, x, xp, xm, lambda i, h: part.at[i, :, h, mid, xr])
+        self.x1f = ring(2, x, xp, xm, lambda i, h: part.at[i, :, h, far, xr])
+        self.y1n = ring(3, y, yp, ym, lambda i, h: part.at[:, i, h, near, yr])
+        self.y1m = ring(4, y, yp, ym, lambda i, h: part.at[:, i, h, mid, yr])
+        self.y1f = ring(5, y, yp, ym, lambda i, h: part.at[:, i, h, far, yr])
+        self.x2n = ring(6, y, yp, ym, lambda i, h: part.at[x, i, h, near, xr])
+        self.x2m = ring(7, y, yp, ym, lambda i, h: part.at[x, i, h, mid, xr])
+        self.x2f = ring(8, y, yp, ym, lambda i, h: part.at[x, i, h, far, xr])
+        self.y2n = ring(9, x, xp, xm, lambda i, h: part.at[i, y, h, near, yr])
+        self.y2m = ring(10, x, xp, xm, lambda i, h: part.at[i, y, h, mid, yr])
+        self.y2f = ring(11, x, xp, xm, lambda i, h: part.at[i, y, h, far, yr])
+        self.z2 = ring(12, x, xp, xm, lambda i, h: part.at[i, quarter(h), zhi, zlo, zr])
+        self.rings = (
+            self.x1n, self.x1m, self.x1f, self.y1n, self.y1m, self.y1f,
+            self.x2n, self.x2m, self.x2f, self.y2n, self.y2m, self.y2f, self.z2,
+        )
+        self.z1 = Ring8(z, zp, zm, lambda i, h: part.at[quarter(h), :, i // 4, i % 4, zr], buf[26], sem[13].at[0], sem[13].at[1])
         self.last_z = []
         for k in range(1, 8):
             high, low = (zhi + k // 4) % 2, ((zlo // 2 + k // 2) % 2) * 2 + (zlo + k) % 2
             self.last_z.append(copy_to(
-                (x * 4 + high * 2 + core, y * 4 + low), part.at[x, y, high, low, self.xy], buf[19].at[k - 1],
-                sem[10].at[0, k], sem[10].at[1, k],
+                (x * 4 + high * 2 + core, y * 4 + low), part.at[x, y, high, low, self.xy], buf[27].at[k - 1],
+                sem[14].at[0, k], sem[14].at[1, k],
             ))
         self.last_y = [
-            copy_to(at_y(y + k), part.at[x, (y + k) % 4, zhi, zlo, zr], buf[20].at[k - 1], sem[11].at[0, k], sem[11].at[1, k])
+            copy_to(at_y(y + k), part.at[x, (y + k) % 4, zhi, zlo, zr], buf[28].at[k - 1], sem[15].at[0, k], sem[15].at[1, k])
             for k in range(1, 4)
         ]
 
-    def start_last_z(self, near):
-        for k in range(1, 8):
-            if (k in (1, 4, 5)) == near:
-                self.last_z[k - 1].start()
+    def start_last_z(self, *ks):
+        for k in ks:
+            self.last_z[k - 1].start()
 
     def start_last_y(self):
         for c in self.last_y:
@@ -162,7 +170,7 @@
 
     def finish_sums(self):
         (row, col, x, y, zhi, zlo, core), _ = self.where
-        for rows, copies, slots in ((self.zr, self.last_y, self.buf[20]), (self.xy, self.last_z, self.buf[19])):
+        for rows, copies, slots in ((self.zr, self.last_y, self.buf[28]), (self.xy, self.last_z, self.buf[27])):
             total = self.part[x, y, zhi, zlo, rows]
             for k, c in enumerate(copies):
                 c.wait_recv()
@@ -171,7 +179,7 @@
 
     def near(self, there, device, k):
         view = self.ar.at[there, self.all]
-        return copy_to(device, view, view, self.sem[12].at[0, k], self.sem[12].at[1, k])
+        return copy_to(device, view, view, self.sem[16].at[0, k], self.sem[16].at[1, k])
 
     def near_send(self, k):
         (row, col, x, y, zhi, zlo, core), _ = self.where
@@ -185,7 +193,7 @@
     def along_y(self, there, j, k):
         (row, col, x, y, zhi, zlo, core), (at_x, at_y, at_z, other) = self.where
         view = self.ar.at[there, self.all]
-        return copy_to(at_y(y + k), view, view, self.sem[13].at[0, j, k], self.sem[13].at[1, j, k])
+        return copy_to(at_y(y + k), view, view, self.sem[17].at[0, j, k], self.sem[17].at[1, j, k])
 
     def along_y_send(self, j, k):
         (row, col, x, y, zhi, zlo, core), _ = self.where
@@ -198,16 +206,16 @@
     def across(self, i):
         (row, col, x, y, zhi, zlo, core), _ = self.where
         device = (((x + i // 2) % 4) * 4 + ((zhi + i % 2) % 2) * 2 + zlo % 2, row)
-        return copy_to(device, self.ar.at[col, self.all], self.ac.at[col, self.all], self.sem[14].at[i], self.sem[15].at[col // 2])
+        return copy_to(device, self.ar.at[col, self.all], self.ac.at[col, self.all], self.sem[18].at[i], self.sem[19].at[col // 2])
 
     def stay(self):
         (row, col, x, y, zhi, zlo, core), _ = self.where
-        return pltpu.make_async_copy(self.ar.at[col, self.all], self.ac.at[col, self.all], self.sem[15].at[col // 2])
+        return pltpu.make_async_copy(self.ar.at[col, self.all], self.ac.at[col, self.all], self.sem[19].at[col // 2])
 
     def hand(self, s):
         (row, col, x, y, zhi, zlo, core), (at_x, at_y, at_z, other) = self.where
         view = self.ac.at[s, self.all]
-        return copy_to(other, view, view, self.sem[16].at[0, s], self.sem[16].at[1, s])
+        return copy_to(other, view, view, self.sem[20].at[0, s], self.sem[20].at[1, s])
 
     def start_gather(self):
         (row, col, x, y, zhi, zlo, core), _ = self.where
@@ -233,32 +241,24 @@
             for k in range(1, 4):
                 self.along_y_send(j, k).start()
 
-    def pass_on(self):
+    def pass_on(self, k):
         (row, col, x, y, zhi, zlo, core), (at_x, at_y, at_z, other) = self.where
-
-        def body(j, carry):
-            s = 2 * j + core
+        for q in range(2):
+            s = (y + 4 - k) % 4 * 4 + 2 * q + core
             view = self.ac.at[s, self.all]
-            copy_to(other, view, view, self.sem[14].at[0], self.sem[15].at[j]).wait_recv()
+            copy_to(other, view, view, self.sem[18].at[0], self.sem[19].at[s // 2]).wait_recv()
             self.hand(s).start()
-            return carry
-
-        lax.fori_loop(0, 8, body, 0)
-
-    def finish_gather(self):
+
+    def arrive(self, k):
         (row, col, x, y, zhi, zlo, core), _ = self.where
         for j in range(4):
-            for k in range(1, 4):
+            if k > 0:
                 self.along_y_recv(j, k).wait_recv()
-
-        def body(j, carry):
-            self.hand(2 * j + 1 - core).wait_recv()
-            return carry
-
-        lax.fori_loop(0, 8, body, 0)
+        for q in range(2):
+            self.hand((y + 4 - k) % 4 * 4 + 2 * q + 1 - core).wait_recv()
 
     def close_sums(self):
-        for ring in (self.x1n, self.x1f, self.y1n, self.y1f, self.z1, self.x2n, self.x2f, self.y2n, self.y2f, self.z2):
+        for ring in self.rings + (self.z1,):
             ring.close()
         for c in self.last_z + self.last_y:
             c.wait_send()
@@ -287,13 +287,14 @@
 def group_buffers(sizes):
     nx, ny, nz = sizes
     one = lambda *lead: [(2,) + lead, (2, 2) + lead]
-    shapes = one(4, 2, nx) * 2 + one(4, 2, ny) * 2 + one(2, nx) * 2 + one(2, ny) * 2 + one(2, nz)
+    shapes = one(4, 2, nx) + one(4, nx) * 2 + one(4, 2, ny) + one(4, ny) * 2
+    shapes += one(2, nx) + one(nx) * 2 + one(2, ny) + one(ny) * 2 + one(2, nz)
     shapes += [(2, 7, 2, 4, nz), (7, nx + ny), (3, nz)]
     return [pltpu.VMEM(s + (128,), jnp.float32) for s in shapes]
 
 
 def group_sems():
-    shapes = [(2, 6)] * 9 + [(2, 2, 7), (2, 8), (2, 4), (2, 4), (2, 4, 4), (8,), (8,), (2, 16)]
+    shapes = [(2, 6)] * 13 + [(2, 2, 7), (2, 8), (2, 4), (2, 4), (2, 4, 4), (8,), (8,), (2, 16)]
     return [pltpu.SemaphoreType.DMA(s) for s in shapes]
 
 
@@ -398,7 +399,7 @@
     groups, first, per = [], 0, len(rest) // len(GROUPS)
     for g, sizes in enumerate(GROUPS):
         own = rest[g * per:(g + 1) * per]
-        groups.append(Group(where, part, ar, ac, first, sizes, own[:21], own[21:]))
+        groups.append(Group(where, part, ar, ac, first, sizes, own[:29], own[29:]))
         first += sum(sizes)
     def step(i, carry):
         take(2 * i)
@@ -413,63 +414,9 @@
         forward(2 * i + 1).wait_recv()
         multiply(i)
 
-    take(1)
-    lax.fori_loop(1, 4, step, 0)
-    drain(3)
-    a, = groups
-    a.x1n.start()
-    a.y1n.start()
-    a.x1n.middle()
-    a.y1n.middle()
-    take(8)
-    take(9)
-    lax.fori_loop(5, 7, step, 0)
-    a.x1n.finish()
-    a.x2n.start()
-    lax.fori_loop(7, 8, step, 0)
-    drain(7)
-    a.x1f.start()
-    a.y1f.start()
-    a.z1.start()
-    a.y1n.finish()
-    a.y2n.start()
-    a.z1.step(2)
-    a.x2n.middle()
-    a.z1.step(3)
-    a.x1f.middle()
-    a.z1.step(4)
-    a.z1.step(5)
-    a.y1f.middle()
-    a.y2n.middle()
-    a.z1.step(6)
-    a.x2n.finish()
-    a.x1f.finish()
-    a.z1.finish()
-    a.y2n.finish()
-    a.x2f.start()
-    a.z2.start()
-    a.start_last_z(True)
-    a.y1f.finish()
-    a.y2f.start()
-    a.z2.middle()
-    a.x2f.middle()
-    a.y2f.middle()
-    a.z2.finish()
-    a.x2f.finish()
-    a.start_last_y()
-    a.y2f.finish()
-    a.start_last_z(False)
-    a.finish_sums()
-    a.start_gather()
-    a.middle_gather()
-    a.pass_on()
-    a.finish_gather()
-    amp_out[...] = ar[col]
-
-
     r_out[...] = jnp.zeros_like(r_out)
 
-    def pair(i, carry):
+    def pair(i):
         a = jnp.concatenate([ar[2 * i], ar[2 * i + 1]], axis=1)
         b = jnp.concatenate([ac[2 * i], ac[2 * i + 1]], axis=1)
         b_hi = b.astype(jnp.bfloat16)
@@ -488,9 +435,80 @@
         one = lax.dot_general(hi, both, contract, preferred_element_type=jnp.float32)
         two = lax.dot_general(lo, b_hi, contract, preferred_element_type=jnp.float32)
         r_out[...] += (one[:, :128] + (one[:, 128:] + two)).reshape(8, 128, 128)
-        return carry
-
-    lax.fori_loop(0, 8, pair, 0)
+
+    a, = groups
+    take(1)
+    lax.fori_loop(1, 4, step, 0)
+    drain(3)
+    a.x1n.start()
+    a.y1n.start()
+    a.x1n.middle()
+    a.y1n.middle()
+    take(8)
+    take(9)
+    step(5, 0)
+    drain(5)
+    a.x1m.start()
+    a.y1m.start()
+    a.x1n.finish()
+    a.x2n.start()
+    take(12)
+    take(13)
+    a.y1n.finish()
+    a.y2n.start()
+    step(7, 0)
+    a.x1m.middle()
+    a.y1m.middle()
+    drain(7)
+    a.z1.start()
+    a.x1f.start()
+    a.y1f.start()
+    a.z1.step(2)
+    a.z1.step(3)
+    a.x2n.middle()
+    a.y2n.middle()
+    a.z1.step(4)
+    a.x1f.middle()
+    a.y1f.middle()
+    a.z1.step(5)
+    a.x1m.finish()
+    a.x2m.start()
+    a.y1m.finish()
+    a.y2m.start()
+    a.z1.step(6)
+    a.x1f.finish()
+    a.x2f.start()
+    a.y1f.finish()
+    a.y2f.start()
+    a.x2n.finish()
+    a.y2n.finish()
+    a.z1.finish()
+    a.z2.start()
+    a.x2m.middle()
+    a.y2m.middle()
+    a.start_last_z(1, 4, 5)
+    a.x2f.middle()
+    a.y2f.middle()
+    a.x2m.finish()
+    a.y2m.finish()
+    a.start_last_z(2, 6)
+    a.z2.middle()
+    a.x2f.finish()
+    a.y2f.finish()
+    a.start_last_z(3, 7)
+    a.z2.finish()
+    a.start_last_y()
+    a.finish_sums()
+    a.start_gather()
+    amp_out[...] = ar[col]
+    a.middle_gather()
+    a.pass_on(0)
+    for k in range(4):
+        if k < 3:
+            a.pass_on(k + 1)
+        a.arrive(k)
+        for q in range(2):
+            pair((y + 4 - k) % 4 * 2 + q)
 
     def close_a2a(j, carry):
         a2a(j).wait_send()

time: 121 us -> 117 us (0.967)
  Pallas kernels: 117 us -> 114 us
    pallas_call x1, Pallas kernels: 117 us -> 114 us  [local(): pl.pallas_call(kernel, out_shape=(jax.ShapeDtypeStruct((128, 128), f32),...]
where the time goes in v4:
time: 117 us
  Pallas kernels  114 us (97%)
  local copies, waits for them, and re-layouts  1.42 us (1%)
    pallas_call x1, Pallas kernels, local(): pl.pallas_call(kernel, out_shape=(jax.ShapeDtypeStruct((128, 128), f32),...  114 us

profile of v4, /device:TPU:7, one launch (start us, length us, event | category | flops | bytes accessed | tf_op | source)
XLA Modules:
  0.0 117.0 jit_solution(10372482025610277349)
XLA Ops:
  0.6 0.8 subtract_divide_fusion.poles
  1.4 114.2 %shard_map.59 = (f32[128,128]{1,0:T(8,128)S(1)}, f32[8,128,128]{2,1,0:T(8,128)S(1)}) custom-call(bf16[464,2048]{1,0:T(8,128)(2,1)} %bitcast.2, bf16[16,464,128]{2,1,0:T(8,128)(2,1)} %bitcast.3, f32[8,2048]{1,0:T(8,128)S(1)} %subtract_divide_fusion.poles), custom_call_target="tpu_custom_call" | custom-call | tf_op jit(solution)/shard_map/pallas_call | solution.py:536
  115.6 0.6 copy.8
  116.3 0.8 copy.9

commit v5 on v4

--- a/solution.py
+++ b/solution.py
@@ -221,6 +221,12 @@
         (row, col, x, y, zhi, zlo, core), _ = self.where
         for k in range(1, 4):
             self.near_send(k).start()
+        for i in (5, 4, 3, 7, 1):
+            self.across(i).start()
+        for k in (2, 1, 3):
+            self.along_y_send(0, k).start()
+        for i in (2, 6):
+            self.across(i).start()
 
         @pl.when(row == col)
         def _():
@@ -230,15 +236,10 @@
         def _():
             self.across(0).start()
 
-        for k in range(1, 4):
-            self.along_y_send(0, k).start()
-        for i in range(1, 8):
-            self.across(i).start()
-
     def middle_gather(self):
         for j in range(1, 4):
             self.near_recv(j).wait_recv()
-            for k in range(1, 4):
+            for k in (2, 1, 3):
                 self.along_y_send(j, k).start()
 
     def pass_on(self, k):

time: 117 us -> 118 us (level); the launches traced: 117 us -> 116 us
  no operation moved by 1% of the time
where the time goes in v5:
time: 118 us; the launch traced here: 116 us
  Pallas kernels  113 us (96%)
  local copies, waits for them, and re-layouts  1.42 us (1%)
    pallas_call x1, Pallas kernels, local(): pl.pallas_call(kernel, out_shape=(jax.ShapeDtypeStruct((128, 128), f32),...  113 us

profile of v5, /device:TPU:7, one launch (start us, length us, event | category | flops | bytes accessed | tf_op | source)
XLA Modules:
  0.0 116.0 jit_solution(4009359021456434907)
XLA Ops:
  0.6 0.8 subtract_divide_fusion.poles
  1.4 113.1 %shard_map.59 = (f32[128,128]{1,0:T(8,128)S(1)}, f32[8,128,128]{2,1,0:T(8,128)S(1)}) custom-call(bf16[464,2048]{1,0:T(8,128)(2,1)} %bitcast.2, bf16[16,464,128]{2,1,0:T(8,128)(2,1)} %bitcast.3, f32[8,2048]{1,0:T(8,128)S(1)} %subtract_divide_fusion.poles), custom_call_target="tpu_custom_call" | custom-call | tf_op jit(solution)/shard_map/pallas_call | solution.py:537
  114.6 0.6 copy.8
  115.2 0.8 copy.9
